TPU v7x, 128 devices: a whole 4x4x4 slice. The times are simulated.
128 devices in a mesh: ctx: 32 (over y, x, core), head: 4 (over z).
Axes of the slice: x: 4, y: 4, z: 4, core: 2. Of those that a mesh axis runs over, the one named last changes fastest.
Arguments:
- q_lin: float32 [8192, 4096], P('ctx', 'head'), may hold values from -6 to 6
- k_lin: float32 [8192, 4096], P('ctx', 'head'), may hold values from -0.9722718 to 0.9722718
- v_lin: float32 [8192, 4096], P('ctx', 'head'), may hold values from -201 to 201
- log_decay: float32 [32, 8192], P('head', 'ctx'), may hold values from -1 to 0
- lin_gain: float32 [4096], P('head'), may hold values from 0.1 to 1.9
- q_soft: float32 [8192, 6144], P('ctx', 'head'), may hold values from -36 to 36
- k_soft: float32 [8192, 1024], P('ctx', 'head'), may hold values from -4 to 4
- v_soft: float32 [8192, 1024], P('ctx', 'head'), may hold values from -6 to 6
Outputs:
- lin_out: float32 [8192, 4096], P('ctx', 'head')
- soft_out: float32 [8192, 6144], P('ctx', 'head')
All inputs are finite; a program needn't handle non-finite values.
Results may differ from a plain program's by a relative error of at most 0.0003.
Values sent between devices are 32-bit elements; how exact they have to be, the bound alone decides.
A program may use at most 128 MiB of HBM per device.

v0:
```python
import math
import jax
import jax.numpy as jnp
from jax import lax
from jax.sharding import PartitionSpec as P

HD = 128
LH = 32
HIGHEST = lax.Precision.HIGHEST
NEGATIVE = -1e30
EPSILON = 1e-05


def entering(value, axis, combine, identity):
    count, mine = (lax.axis_size(axis), lax.axis_index(axis))
    everything = jax.tree.map(lambda part: lax.all_gather(part, axis), value)
    start = jax.tree.map(
        lambda part, zero: jnp.broadcast_to(jnp.asarray(zero, part.dtype), part.shape),
        value,
        identity,
    )

    def turn(k, before):
        reached = k < mine
        new = combine(before, jax.tree.map(lambda part: part[k], everything))
        return jax.tree.map(lambda a, b: jnp.where(reached, a, b), new, before)

    return lax.fori_loop(0, count, turn, start)


def block_terms(queries, key_rows, value_rows, log_rates):
    length = queries.shape[0]
    cumulative = jnp.cumsum(log_rates, axis=1)
    positions = jnp.arange(length)
    causal = (positions[:, None] >= positions[None, :])[None]
    decay_gaps = cumulative[:, :, None] - cumulative[:, None, :]
    weights = jnp.where(causal, jnp.exp(jnp.where(causal, decay_gaps, 0.0)), 0.0)
    scores = jnp.einsum("thd,shd->hts", queries, key_rows, precision=HIGHEST)
    inside = jnp.einsum("hts,shd->thd", scores * weights, value_rows, precision=HIGHEST)
    block_total = cumulative[:, -1]
    trailing = jnp.exp(block_total[:, None] - cumulative)
    scaled_keys = key_rows * jnp.transpose(trailing)[:, :, None]
    local_state = jnp.einsum("shd,she->hde", scaled_keys, value_rows, precision=HIGHEST)
    leading = jnp.transpose(jnp.exp(cumulative))[:, :, None]
    return (inside, leading, block_total, local_state)


def attend(partial_value, query_rows, query_pos, key_slab, value_slab, key_pos, score_scale):
    old_max, old_total, weighted = partial_value
    scores = jnp.einsum("tkgd,skd->kgts", query_rows, key_slab, precision=HIGHEST) * score_scale
    visible = (key_pos[None, :] <= query_pos[:, None])[None, None]
    scores = jnp.where(visible, scores, NEGATIVE)
    new_max = jnp.maximum(old_max, jnp.max(scores, axis=3))
    weights = jnp.where(visible, jnp.exp(scores - new_max[..., None]), 0.0)
    shrink = jnp.exp(old_max - new_max)
    new_total = old_total * shrink + jnp.sum(weights, axis=3)
    weighted = weighted * shrink[..., None] + jnp.einsum(
        "kgts,skd->kgtd", weights, value_slab, precision=HIGHEST
    )
    return (new_max, new_total, weighted)


def soft_layer(query_sets, k_soft, v_soft, score_scale):
    kv_heads = k_soft.shape[1] // HD
    initial = []
    for query_rows, query_pos in query_sets:
        shape = (query_rows.shape[1], query_rows.shape[2], query_rows.shape[0])
        initial.append(
            (
                jnp.full(shape, NEGATIVE, jnp.float32),
                jnp.zeros(shape, jnp.float32),
                jnp.zeros(shape + (HD,), jnp.float32),
            )
        )
    initial = tuple(initial)
    key_rows = lax.all_gather(k_soft, "ctx", axis=0, tiled=True)
    value_rows = lax.all_gather(v_soft, "ctx", axis=0, tiled=True)
    shard_rows = key_rows.shape[0]
    key_block = math.gcd(shard_rows, 512)
    key_rows = key_rows.reshape(shard_rows // key_block, key_block, kv_heads, HD)
    value_rows = value_rows.reshape(shard_rows // key_block, key_block, kv_heads, HD)

    def visit(block_index, partials):
        key_slab = lax.dynamic_index_in_dim(key_rows, block_index, 0, keepdims=False)
        value_slab = lax.dynamic_index_in_dim(value_rows, block_index, 0, keepdims=False)
        first_key = block_index * key_block
        key_pos = first_key + jnp.arange(key_block)
        updated = []
        for (query_rows, query_pos), partial_value in zip(query_sets, partials):

            def engage(current, query_rows=query_rows, query_pos=query_pos):
                return attend(
                    current, query_rows, query_pos, key_slab, value_slab, key_pos, score_scale
                )

            def remain(current):
                return current

            updated.append(lax.cond(first_key <= jnp.max(query_pos), engage, remain, partial_value))
        return tuple(updated)

    finals = lax.fori_loop(0, shard_rows // key_block, visit, initial)
    results = []
    for final in finals:
        maxima, totals, weighted = final
        merged = weighted / totals[..., None]
        row_count = merged.shape[2]
        results.append(jnp.transpose(merged, (2, 0, 1, 3)).reshape(row_count, -1))
    return results


def body(q_lin, k_lin, v_lin, log_decay, lin_gain, q_soft, k_soft, v_soft):
    row_count = q_lin.shape[0]
    head_count = log_decay.shape[0]
    position = lax.axis_index("ctx")
    queries = q_lin.reshape(row_count, head_count, HD)
    key_rows = k_lin.reshape(row_count, head_count, HD)
    value_rows = v_lin.reshape(row_count, head_count, HD)
    inside, leading, block_total, local_state = block_terms(
        queries, key_rows, value_rows, log_decay
    )

    def chain_step(earlier, later):
        return (earlier[0] + later[0], jnp.exp(later[0])[:, None, None] * earlier[1] + later[1])

    identity = (jnp.zeros_like(block_total), jnp.zeros_like(local_state))
    prefix_pair = entering((block_total, local_state), "ctx", chain_step, identity)
    prior_state = prefix_pair[1]
    linear = inside + leading * jnp.einsum("thd,hde->the", queries, prior_state, precision=HIGHEST)
    linear = linear.reshape(row_count, head_count * HD)
    energy = lax.psum(jnp.sum(linear * linear, axis=1, keepdims=True), "head")
    lin_out = linear * lax.rsqrt(energy / (LH * HD) + EPSILON) * lin_gain
    score_scale = 1.0 / math.sqrt(HD)
    kv_heads = k_soft.shape[1] // HD
    group_size = q_soft.shape[1] // (kv_heads * HD)
    soft_queries = q_soft.reshape(row_count, kv_heads, group_size, HD)
    query_pos = position * row_count + jnp.arange(row_count)
    soft_out = soft_layer([(soft_queries, query_pos)], k_soft, v_soft, score_scale)[0]
    return (lin_out, soft_out)


def solution(mesh):
    return jax.shard_map(
        body,
        mesh=mesh,
        in_specs=(
            P("ctx", "head"),
            P("ctx", "head"),
            P("ctx", "head"),
            P("head", "ctx"),
            P("head"),
            P("ctx", "head"),
            P("ctx", "head"),
            P("ctx", "head"),
        ),
        out_specs=(P("ctx", "head"), P("ctx", "head")),
        check_vma=False,
    )
```

profile of v0, /device:TPU:30, one launch (start us, length us, event | category | flops | bytes accessed | tf_op | source)
XLA Modules:
  0.0 573.1 jit_solution(4927016760311225648)
XLA Ops:
  17.5 59.2 %all-reduce = f32[256]{0:T(256)S(1)} all-reduce(f32[256]{0:T(256)S(1)} %dynamic-update-slice), channel_id=2, replica_groups=mesh['ctx'=32,'head'=4] {'ctx'}, use_global_device_ids=true, to_apply=%add | all-reduce | flops 256 | bytes 2048
  137.9 363.9 %while.33 = (s32[]{:T(128)}, f32[2,6,256]{2,1,0:T(8,128)S(1)}, f32[2,6,256]{2,1,0:T(8,128)S(1)}, f32[2,6,256,128]{3,2,1,0:T(8,128)}, s32[]{:T(128)}, /*index=5*/...) while((s32[]{:T(128)}, f32[2,6,256]{2,1,0:T(8,128)S(1)}, ...), condition=%wide.region_12.13_spmd.clone, body=%wide.region_7.0_spmd.clone.sunk | while | flops 4851637248 | bytes 37959000 | solution.py:102
  138.4 22.2 %conditional.3 = ((f32[2,6,256]{2,1,0:T(8,128)S(1)}, f32[2,6,256]{2,1,0:T(8,128)S(1)}, f32[2,6,256,128]{3,2,1,0:T(8,128)})) conditional(s32[]{:T(128)} %convert_element_type.10, (f32[2,6,256]{2,1,0:T(8,128)S(1)}, f32[2,6,256]{2,1,0:T(8,128)S(1)}, f32[2,6,256,128]{3,2,1,0:T(8,128)}) %tuple.98, (s32[]{:T(128)}, s32[512]{0:T(512)S(1)}, s32[]{:T(128)}, ...), branch_computations={%region_8.8_spmd, %region_9.11_spmd} | conditional | flops 4851637248 | bytes 37955680 | solution.py:99
  147.2 12.2 %multiply_add_fusion = f32[2,6,256,128]{3,2,1,0:T(8,128)S(1)} fusion(f32[2,6,256,128]{3,2,1,0:T(8,128)S(1)} %copy-done.2, f32[2,512,256,6]{2,1,3,0:T(8,128)S(1)} %get-tuple-element.535, f32[2,6,256]{2,1,0:T(8,128)S(1)} %max.6, pred[256,512]{0,1:T(8,128)(4,1)S(1)} %broadcast_compare_fusion, f32[2,6,256]{2,1,0:T(8,128)S(1)} %get-tuple-element.531, ...), kind=kOutput, calls=%fused_computation.11 | convolution fusion | flops 2422996992 | bytes 10117632 | tf_op jit(solution)/shard_map/while/body/eval_jaxpr/cond/branch_1_fun/kgts,skd->kgtd/dot_general | solution.py:57
  161.2 22.2 %conditional.3 = ((f32[2,6,256]{2,1,0:T(8,128)S(1)}, f32[2,6,256]{2,1,0:T(8,128)S(1)}, f32[2,6,256,128]{3,2,1,0:T(8,128)})) conditional(s32[]{:T(128)} %convert_element_type.10, (f32[2,6,256]{2,1,0:T(8,128)S(1)}, f32[2,6,256]{2,1,0:T(8,128)S(1)}, f32[2,6,256,128]{3,2,1,0:T(8,128)}) %tuple.98, (s32[]{:T(128)}, s32[512]{0:T(512)S(1)}, s32[]{:T(128)}, ...), branch_computations={%region_8.8_spmd, %region_9.11_spmd} | conditional | flops 4851637248 | bytes 37955680 | solution.py:99
  170.0 12.2 %multiply_add_fusion = f32[2,6,256,128]{3,2,1,0:T(8,128)S(1)} fusion(f32[2,6,256,128]{3,2,1,0:T(8,128)S(1)} %copy-done.2, f32[2,512,256,6]{2,1,3,0:T(8,128)S(1)} %get-tuple-element.535, f32[2,6,256]{2,1,0:T(8,128)S(1)} %max.6, pred[256,512]{0,1:T(8,128)(4,1)S(1)} %broadcast_compare_fusion, f32[2,6,256]{2,1,0:T(8,128)S(1)} %get-tuple-element.531, ...), kind=kOutput, calls=%fused_computation.11 | convolution fusion | flops 2422996992 | bytes 10117632 | tf_op jit(solution)/shard_map/while/body/eval_jaxpr/cond/branch_1_fun/kgts,skd->kgtd/dot_general | solution.py:57
  183.9 22.2 %conditional.3 = ((f32[2,6,256]{2,1,0:T(8,128)S(1)}, f32[2,6,256]{2,1,0:T(8,128)S(1)}, f32[2,6,256,128]{3,2,1,0:T(8,128)})) conditional(s32[]{:T(128)} %convert_element_type.10, (f32[2,6,256]{2,1,0:T(8,128)S(1)}, f32[2,6,256]{2,1,0:T(8,128)S(1)}, f32[2,6,256,128]{3,2,1,0:T(8,128)}) %tuple.98, (s32[]{:T(128)}, s32[512]{0:T(512)S(1)}, s32[]{:T(128)}, ...), branch_computations={%region_8.8_spmd, %region_9.11_spmd} | conditional | flops 4851637248 | bytes 37955680 | solution.py:99
  192.7 12.2 %multiply_add_fusion = f32[2,6,256,128]{3,2,1,0:T(8,128)S(1)} fusion(f32[2,6,256,128]{3,2,1,0:T(8,128)S(1)} %copy-done.2, f32[2,512,256,6]{2,1,3,0:T(8,128)S(1)} %get-tuple-element.535, f32[2,6,256]{2,1,0:T(8,128)S(1)} %max.6, pred[256,512]{0,1:T(8,128)(4,1)S(1)} %broadcast_compare_fusion, f32[2,6,256]{2,1,0:T(8,128)S(1)} %get-tuple-element.531, ...), kind=kOutput, calls=%fused_computation.11 | convolution fusion | flops 2422996992 | bytes 10117632 | tf_op jit(solution)/shard_map/while/body/eval_jaxpr/cond/branch_1_fun/kgts,skd->kgtd/dot_general | solution.py:57
  206.7 22.2 %conditional.3 = ((f32[2,6,256]{2,1,0:T(8,128)S(1)}, f32[2,6,256]{2,1,0:T(8,128)S(1)}, f32[2,6,256,128]{3,2,1,0:T(8,128)})) conditional(s32[]{:T(128)} %convert_element_type.10, (f32[2,6,256]{2,1,0:T(8,128)S(1)}, f32[2,6,256]{2,1,0:T(8,128)S(1)}, f32[2,6,256,128]{3,2,1,0:T(8,128)}) %tuple.98, (s32[]{:T(128)}, s32[512]{0:T(512)S(1)}, s32[]{:T(128)}, ...), branch_computations={%region_8.8_spmd, %region_9.11_spmd} | conditional | flops 4851637248 | bytes 37955680 | solution.py:99
  215.5 12.2 %multiply_add_fusion = f32[2,6,256,128]{3,2,1,0:T(8,128)S(1)} fusion(f32[2,6,256,128]{3,2,1,0:T(8,128)S(1)} %copy-done.2, f32[2,512,256,6]{2,1,3,0:T(8,128)S(1)} %get-tuple-element.535, f32[2,6,256]{2,1,0:T(8,128)S(1)} %max.6, pred[256,512]{0,1:T(8,128)(4,1)S(1)} %broadcast_compare_fusion, f32[2,6,256]{2,1,0:T(8,128)S(1)} %get-tuple-element.531, ...), kind=kOutput, calls=%fused_computation.11 | convolution fusion | flops 2422996992 | bytes 10117632 | tf_op jit(solution)/shard_map/while/body/eval_jaxpr/cond/branch_1_fun/kgts,skd->kgtd/dot_general | solution.py:57
  229.4 22.2 %conditional.3 = ((f32[2,6,256]{2,1,0:T(8,128)S(1)}, f32[2,6,256]{2,1,0:T(8,128)S(1)}, f32[2,6,256,128]{3,2,1,0:T(8,128)})) conditional(s32[]{:T(128)} %convert_element_type.10, (f32[2,6,256]{2,1,0:T(8,128)S(1)}, f32[2,6,256]{2,1,0:T(8,128)S(1)}, f32[2,6,256,128]{3,2,1,0:T(8,128)}) %tuple.98, (s32[]{:T(128)}, s32[512]{0:T(512)S(1)}, s32[]{:T(128)}, ...), branch_computations={%region_8.8_spmd, %region_9.11_spmd} | conditional | flops 4851637248 | bytes 37955680 | solution.py:99
  238.2 12.2 %multiply_add_fusion = f32[2,6,256,128]{3,2,1,0:T(8,128)S(1)} fusion(f32[2,6,256,128]{3,2,1,0:T(8,128)S(1)} %copy-done.2, f32[2,512,256,6]{2,1,3,0:T(8,128)S(1)} %get-tuple-element.535, f32[2,6,256]{2,1,0:T(8,128)S(1)} %max.6, pred[256,512]{0,1:T(8,128)(4,1)S(1)} %broadcast_compare_fusion, f32[2,6,256]{2,1,0:T(8,128)S(1)} %get-tuple-element.531, ...), kind=kOutput, calls=%fused_computation.11 | convolution fusion | flops 2422996992 | bytes 10117632 | tf_op jit(solution)/shard_map/while/body/eval_jaxpr/cond/branch_1_fun/kgts,skd->kgtd/dot_general | solution.py:57
  252.2 22.2 %conditional.3 = ((f32[2,6,256]{2,1,0:T(8,128)S(1)}, f32[2,6,256]{2,1,0:T(8,128)S(1)}, f32[2,6,256,128]{3,2,1,0:T(8,128)})) conditional(s32[]{:T(128)} %convert_element_type.10, (f32[2,6,256]{2,1,0:T(8,128)S(1)}, f32[2,6,256]{2,1,0:T(8,128)S(1)}, f32[2,6,256,128]{3,2,1,0:T(8,128)}) %tuple.98, (s32[]{:T(128)}, s32[512]{0:T(512)S(1)}, s32[]{:T(128)}, ...), branch_computations={%region_8.8_spmd, %region_9.11_spmd} | conditional | flops 4851637248 | bytes 37955680 | solution.py:99
  261.0 12.2 %multiply_add_fusion = f32[2,6,256,128]{3,2,1,0:T(8,128)S(1)} fusion(f32[2,6,256,128]{3,2,1,0:T(8,128)S(1)} %copy-done.2, f32[2,512,256,6]{2,1,3,0:T(8,128)S(1)} %get-tuple-element.535, f32[2,6,256]{2,1,0:T(8,128)S(1)} %max.6, pred[256,512]{0,1:T(8,128)(4,1)S(1)} %broadcast_compare_fusion, f32[2,6,256]{2,1,0:T(8,128)S(1)} %get-tuple-element.531, ...), kind=kOutput, calls=%fused_computation.11 | convolution fusion | flops 2422996992 | bytes 10117632 | tf_op jit(solution)/shard_map/while/body/eval_jaxpr/cond/branch_1_fun/kgts,skd->kgtd/dot_general | solution.py:57
  274.9 22.2 %conditional.3 = ((f32[2,6,256]{2,1,0:T(8,128)S(1)}, f32[2,6,256]{2,1,0:T(8,128)S(1)}, f32[2,6,256,128]{3,2,1,0:T(8,128)})) conditional(s32[]{:T(128)} %convert_element_type.10, (f32[2,6,256]{2,1,0:T(8,128)S(1)}, f32[2,6,256]{2,1,0:T(8,128)S(1)}, f32[2,6,256,128]{3,2,1,0:T(8,128)}) %tuple.98, (s32[]{:T(128)}, s32[512]{0:T(512)S(1)}, s32[]{:T(128)}, ...), branch_computations={%region_8.8_spmd, %region_9.11_spmd} | conditional | flops 4851637248 | bytes 37955680 | solution.py:99
  283.7 12.2 %multiply_add_fusion = f32[2,6,256,128]{3,2,1,0:T(8,128)S(1)} fusion(f32[2,6,256,128]{3,2,1,0:T(8,128)S(1)} %copy-done.2, f32[2,512,256,6]{2,1,3,0:T(8,128)S(1)} %get-tuple-element.535, f32[2,6,256]{2,1,0:T(8,128)S(1)} %max.6, pred[256,512]{0,1:T(8,128)(4,1)S(1)} %broadcast_compare_fusion, f32[2,6,256]{2,1,0:T(8,128)S(1)} %get-tuple-element.531, ...), kind=kOutput, calls=%fused_computation.11 | convolution fusion | flops 2422996992 | bytes 10117632 | tf_op jit(solution)/shard_map/while/body/eval_jaxpr/cond/branch_1_fun/kgts,skd->kgtd/dot_general | solution.py:57
  297.6 22.2 %conditional.3 = ((f32[2,6,256]{2,1,0:T(8,128)S(1)}, f32[2,6,256]{2,1,0:T(8,128)S(1)}, f32[2,6,256,128]{3,2,1,0:T(8,128)})) conditional(s32[]{:T(128)} %convert_element_type.10, (f32[2,6,256]{2,1,0:T(8,128)S(1)}, f32[2,6,256]{2,1,0:T(8,128)S(1)}, f32[2,6,256,128]{3,2,1,0:T(8,128)}) %tuple.98, (s32[]{:T(128)}, s32[512]{0:T(512)S(1)}, s32[]{:T(128)}, ...), branch_computations={%region_8.8_spmd, %region_9.11_spmd} | conditional | flops 4851637248 | bytes 37955680 | solution.py:99
  306.4 12.2 %multiply_add_fusion = f32[2,6,256,128]{3,2,1,0:T(8,128)S(1)} fusion(f32[2,6,256,128]{3,2,1,0:T(8,128)S(1)} %copy-done.2, f32[2,512,256,6]{2,1,3,0:T(8,128)S(1)} %get-tuple-element.535, f32[2,6,256]{2,1,0:T(8,128)S(1)} %max.6, pred[256,512]{0,1:T(8,128)(4,1)S(1)} %broadcast_compare_fusion, f32[2,6,256]{2,1,0:T(8,128)S(1)} %get-tuple-element.531, ...), kind=kOutput, calls=%fused_computation.11 | convolution fusion | flops 2422996992 | bytes 10117632 | tf_op jit(solution)/shard_map/while/body/eval_jaxpr/cond/branch_1_fun/kgts,skd->kgtd/dot_general | solution.py:57
  320.4 22.2 %conditional.3 = ((f32[2,6,256]{2,1,0:T(8,128)S(1)}, f32[2,6,256]{2,1,0:T(8,128)S(1)}, f32[2,6,256,128]{3,2,1,0:T(8,128)})) conditional(s32[]{:T(128)} %convert_element_type.10, (f32[2,6,256]{2,1,0:T(8,128)S(1)}, f32[2,6,256]{2,1,0:T(8,128)S(1)}, f32[2,6,256,128]{3,2,1,0:T(8,128)}) %tuple.98, (s32[]{:T(128)}, s32[512]{0:T(512)S(1)}, s32[]{:T(128)}, ...), branch_computations={%region_8.8_spmd, %region_9.11_spmd} | conditional | flops 4851637248 | bytes 37955680 | solution.py:99
  329.2 12.2 %multiply_add_fusion = f32[2,6,256,128]{3,2,1,0:T(8,128)S(1)} fusion(f32[2,6,256,128]{3,2,1,0:T(8,128)S(1)} %copy-done.2, f32[2,512,256,6]{2,1,3,0:T(8,128)S(1)} %get-tuple-element.535, f32[2,6,256]{2,1,0:T(8,128)S(1)} %max.6, pred[256,512]{0,1:T(8,128)(4,1)S(1)} %broadcast_compare_fusion, f32[2,6,256]{2,1,0:T(8,128)S(1)} %get-tuple-element.531, ...), kind=kOutput, calls=%fused_computation.11 | convolution fusion | flops 2422996992 | bytes 10117632 | tf_op jit(solution)/shard_map/while/body/eval_jaxpr/cond/branch_1_fun/kgts,skd->kgtd/dot_general | solution.py:57
  343.1 22.2 %conditional.3 = ((f32[2,6,256]{2,1,0:T(8,128)S(1)}, f32[2,6,256]{2,1,0:T(8,128)S(1)}, f32[2,6,256,128]{3,2,1,0:T(8,128)})) conditional(s32[]{:T(128)} %convert_element_type.10, (f32[2,6,256]{2,1,0:T(8,128)S(1)}, f32[2,6,256]{2,1,0:T(8,128)S(1)}, f32[2,6,256,128]{3,2,1,0:T(8,128)}) %tuple.98, (s32[]{:T(128)}, s32[512]{0:T(512)S(1)}, s32[]{:T(128)}, ...), branch_computations={%region_8.8_spmd, %region_9.11_spmd} | conditional | flops 4851637248 | bytes 37955680 | solution.py:99
  351.9 12.2 %multiply_add_fusion = f32[2,6,256,128]{3,2,1,0:T(8,128)S(1)} fusion(f32[2,6,256,128]{3,2,1,0:T(8,128)S(1)} %copy-done.2, f32[2,512,256,6]{2,1,3,0:T(8,128)S(1)} %get-tuple-element.535, f32[2,6,256]{2,1,0:T(8,128)S(1)} %max.6, pred[256,512]{0,1:T(8,128)(4,1)S(1)} %broadcast_compare_fusion, f32[2,6,256]{2,1,0:T(8,128)S(1)} %get-tuple-element.531, ...), kind=kOutput, calls=%fused_computation.11 | convolution fusion | flops 2422996992 | bytes 10117632 | tf_op jit(solution)/shard_map/while/body/eval_jaxpr/cond/branch_1_fun/kgts,skd->kgtd/dot_general | solution.py:57
  365.9 22.2 %conditional.3 = ((f32[2,6,256]{2,1,0:T(8,128)S(1)}, f32[2,6,256]{2,1,0:T(8,128)S(1)}, f32[2,6,256,128]{3,2,1,0:T(8,128)})) conditional(s32[]{:T(128)} %convert_element_type.10, (f32[2,6,256]{2,1,0:T(8,128)S(1)}, f32[2,6,256]{2,1,0:T(8,128)S(1)}, f32[2,6,256,128]{3,2,1,0:T(8,128)}) %tuple.98, (s32[]{:T(128)}, s32[512]{0:T(512)S(1)}, s32[]{:T(128)}, ...), branch_computations={%region_8.8_spmd, %region_9.11_spmd} | conditional | flops 4851637248 | bytes 37955680 | solution.py:99
  374.7 12.2 %multiply_add_fusion = f32[2,6,256,128]{3,2,1,0:T(8,128)S(1)} fusion(f32[2,6,256,128]{3,2,1,0:T(8,128)S(1)} %copy-done.2, f32[2,512,256,6]{2,1,3,0:T(8,128)S(1)} %get-tuple-element.535, f32[2,6,256]{2,1,0:T(8,128)S(1)} %max.6, pred[256,512]{0,1:T(8,128)(4,1)S(1)} %broadcast_compare_fusion, f32[2,6,256]{2,1,0:T(8,128)S(1)} %get-tuple-element.531, ...), kind=kOutput, calls=%fused_computation.11 | convolution fusion | flops 2422996992 | bytes 10117632 | tf_op jit(solution)/shard_map/while/body/eval_jaxpr/cond/branch_1_fun/kgts,skd->kgtd/dot_general | solution.py:57
  388.6 22.2 %conditional.3 = ((f32[2,6,256]{2,1,0:T(8,128)S(1)}, f32[2,6,256]{2,1,0:T(8,128)S(1)}, f32[2,6,256,128]{3,2,1,0:T(8,128)})) conditional(s32[]{:T(128)} %convert_element_type.10, (f32[2,6,256]{2,1,0:T(8,128)S(1)}, f32[2,6,256]{2,1,0:T(8,128)S(1)}, f32[2,6,256,128]{3,2,1,0:T(8,128)}) %tuple.98, (s32[]{:T(128)}, s32[512]{0:T(512)S(1)}, s32[]{:T(128)}, ...), branch_computations={%region_8.8_spmd, %region_9.11_spmd} | conditional | flops 4851637248 | bytes 37955680 | solution.py:99
  397.4 12.2 %multiply_add_fusion = f32[2,6,256,128]{3,2,1,0:T(8,128)S(1)} fusion(f32[2,6,256,128]{3,2,1,0:T(8,128)S(1)} %copy-done.2, f32[2,512,256,6]{2,1,3,0:T(8,128)S(1)} %get-tuple-element.535, f32[2,6,256]{2,1,0:T(8,128)S(1)} %max.6, pred[256,512]{0,1:T(8,128)(4,1)S(1)} %broadcast_compare_fusion, f32[2,6,256]{2,1,0:T(8,128)S(1)} %get-tuple-element.531, ...), kind=kOutput, calls=%fused_computation.11 | convolution fusion | flops 2422996992 | bytes 10117632 | tf_op jit(solution)/shard_map/while/body/eval_jaxpr/cond/branch_1_fun/kgts,skd->kgtd/dot_general | solution.py:57
  411.3 22.2 %conditional.3 = ((f32[2,6,256]{2,1,0:T(8,128)S(1)}, f32[2,6,256]{2,1,0:T(8,128)S(1)}, f32[2,6,256,128]{3,2,1,0:T(8,128)})) conditional(s32[]{:T(128)} %convert_element_type.10, (f32[2,6,256]{2,1,0:T(8,128)S(1)}, f32[2,6,256]{2,1,0:T(8,128)S(1)}, f32[2,6,256,128]{3,2,1,0:T(8,128)}) %tuple.98, (s32[]{:T(128)}, s32[512]{0:T(512)S(1)}, s32[]{:T(128)}, ...), branch_computations={%region_8.8_spmd, %region_9.11_spmd} | conditional | flops 4851637248 | bytes 37955680 | solution.py:99
  420.1 12.2 %multiply_add_fusion = f32[2,6,256,128]{3,2,1,0:T(8,128)S(1)} fusion(f32[2,6,256,128]{3,2,1,0:T(8,128)S(1)} %copy-done.2, f32[2,512,256,6]{2,1,3,0:T(8,128)S(1)} %get-tuple-element.535, f32[2,6,256]{2,1,0:T(8,128)S(1)} %max.6, pred[256,512]{0,1:T(8,128)(4,1)S(1)} %broadcast_compare_fusion, f32[2,6,256]{2,1,0:T(8,128)S(1)} %get-tuple-element.531, ...), kind=kOutput, calls=%fused_computation.11 | convolution fusion | flops 2422996992 | bytes 10117632 | tf_op jit(solution)/shard_map/while/body/eval_jaxpr/cond/branch_1_fun/kgts,skd->kgtd/dot_general | solution.py:57
  434.1 22.2 %conditional.3 = ((f32[2,6,256]{2,1,0:T(8,128)S(1)}, f32[2,6,256]{2,1,0:T(8,128)S(1)}, f32[2,6,256,128]{3,2,1,0:T(8,128)})) conditional(s32[]{:T(128)} %convert_element_type.10, (f32[2,6,256]{2,1,0:T(8,128)S(1)}, f32[2,6,256]{2,1,0:T(8,128)S(1)}, f32[2,6,256,128]{3,2,1,0:T(8,128)}) %tuple.98, (s32[]{:T(128)}, s32[512]{0:T(512)S(1)}, s32[]{:T(128)}, ...), branch_computations={%region_8.8_spmd, %region_9.11_spmd} | conditional | flops 4851637248 | bytes 37955680 | solution.py:99
  456.8 22.2 %conditional.3 = ((f32[2,6,256]{2,1,0:T(8,128)S(1)}, f32[2,6,256]{2,1,0:T(8,128)S(1)}, f32[2,6,256,128]{3,2,1,0:T(8,128)})) conditional(s32[]{:T(128)} %convert_element_type.10, (f32[2,6,256]{2,1,0:T(8,128)S(1)}, f32[2,6,256]{2,1,0:T(8,128)S(1)}, f32[2,6,256,128]{3,2,1,0:T(8,128)}) %tuple.98, (s32[]{:T(128)}, s32[512]{0:T(512)S(1)}, s32[]{:T(128)}, ...), branch_computations={%region_8.8_spmd, %region_9.11_spmd} | conditional | flops 4851637248 | bytes 37955680 | solution.py:99
  479.6 22.2 %conditional.3 = ((f32[2,6,256]{2,1,0:T(8,128)S(1)}, f32[2,6,256]{2,1,0:T(8,128)S(1)}, f32[2,6,256,128]{3,2,1,0:T(8,128)})) conditional(s32[]{:T(128)} %convert_element_type.10, (f32[2,6,256]{2,1,0:T(8,128)S(1)}, f32[2,6,256]{2,1,0:T(8,128)S(1)}, f32[2,6,256,128]{3,2,1,0:T(8,128)}) %tuple.98, (s32[]{:T(128)}, s32[512]{0:T(512)S(1)}, s32[]{:T(128)}, ...), branch_computations={%region_8.8_spmd, %region_9.11_spmd} | conditional | flops 4851637248 | bytes 37955680 | solution.py:99
  508.1 38.9 %while.34 = (s32[]{:T(128)}, f32[8,128,128]{2,1,0:T(8,128)S(1)}, s32[]{:T(128)}, f32[32,8]{1,0:T(8,128)S(1)}, f32[32,8,128,128]{3,2,1,0:T(8,128)}, /*index=5*/s32[]{:T(128)}, s32[]{:T(128)}) while((s32[]{:T(128)}, f32[8,128,128]{2,1,0:T(8,128)S(1)}, s32[]{:T(128)}, f32[32,8]{1,0:T(8,128)S(1)}, f32[32,8,128,128]{3,2,1,0:T(8,128)}, ...), condition=%wide.region_3.4_spmd.clone, body=%wide.region_2.3_spmd.clone.sunk | while | flops 524292 | bytes 1573065 | solution.py:28
  (343 shorter events, 328.8 us)
Async XLA Ops:
  7.2 75.3 %copy-start = (f32[256,1024]{1,0:T(8,128)S(1)}, f32[256,1024]{1,0:T(8,128)}, u32[]{:S(2)}) copy-start(f32[256,1024]{1,0:T(8,128)} %param.14) | copy-start | bytes 3145732
  7.2 79.7 %all-gather.6.cloned.1.call-start = ((), (), s32[]{:S(2)}) async-start(), calls=%async_computation | async-start | bytes 8650752 | tf_op jit(solution)/shard_map/all_gather | solution.py:76
  7.9 110.0 %all-gather.8.cloned.1.call-start = ((), (), s32[]{:S(2)}) async-start(), calls=%async_computation.1 | async-start | bytes 8650752 | tf_op jit(solution)/shard_map/all_gather | solution.py:77
  8.7 499.4 %all-gather.10.cloned.1.call-start = ((), (), s32[]{:S(2)}) async-start(), calls=%async_computation.2 | async-start | bytes 17301504 | tf_op jit(solution)/shard_map/all_gather | solution.py:16
  11.7 3.6 copy-start.1
  138.6 8.6 %copy-start.2 = (f32[2,6,256,128]{3,2,1,0:T(8,128)S(1)}, f32[2,6,256,128]{3,2,1,0:T(8,128)}, u32[]{:S(2)}) copy-start(f32[2,6,256,128]{3,2,1,0:T(8,128)} %get-tuple-element.401) | copy-start | bytes 4718596 | tf_op jit(solution)/shard_map/while/body/eval_jaxpr/cond
  159.5 1.1 copy-start.3
  161.4 8.6 %copy-start.2 = (f32[2,6,256,128]{3,2,1,0:T(8,128)S(1)}, f32[2,6,256,128]{3,2,1,0:T(8,128)}, u32[]{:S(2)}) copy-start(f32[2,6,256,128]{3,2,1,0:T(8,128)} %get-tuple-element.401) | copy-start | bytes 4718596 | tf_op jit(solution)/shard_map/while/body/eval_jaxpr/cond
  182.2 1.1 copy-start.3
  184.1 8.6 %copy-start.2 = (f32[2,6,256,128]{3,2,1,0:T(8,128)S(1)}, f32[2,6,256,128]{3,2,1,0:T(8,128)}, u32[]{:S(2)}) copy-start(f32[2,6,256,128]{3,2,1,0:T(8,128)} %get-tuple-element.401) | copy-start | bytes 4718596 | tf_op jit(solution)/shard_map/while/body/eval_jaxpr/cond
  205.0 1.1 copy-start.3
  206.9 8.6 %copy-start.2 = (f32[2,6,256,128]{3,2,1,0:T(8,128)S(1)}, f32[2,6,256,128]{3,2,1,0:T(8,128)}, u32[]{:S(2)}) copy-start(f32[2,6,256,128]{3,2,1,0:T(8,128)} %get-tuple-element.401) | copy-start | bytes 4718596 | tf_op jit(solution)/shard_map/while/body/eval_jaxpr/cond
  227.7 1.1 copy-start.3
  229.6 8.6 %copy-start.2 = (f32[2,6,256,128]{3,2,1,0:T(8,128)S(1)}, f32[2,6,256,128]{3,2,1,0:T(8,128)}, u32[]{:S(2)}) copy-start(f32[2,6,256,128]{3,2,1,0:T(8,128)} %get-tuple-element.401) | copy-start | bytes 4718596 | tf_op jit(solution)/shard_map/while/body/eval_jaxpr/cond
  250.4 1.1 copy-start.3
  252.4 8.6 %copy-start.2 = (f32[2,6,256,128]{3,2,1,0:T(8,128)S(1)}, f32[2,6,256,128]{3,2,1,0:T(8,128)}, u32[]{:S(2)}) copy-start(f32[2,6,256,128]{3,2,1,0:T(8,128)} %get-tuple-element.401) | copy-start | bytes 4718596 | tf_op jit(solution)/shard_map/while/body/eval_jaxpr/cond
  273.2 1.1 copy-start.3
  275.1 8.6 %copy-start.2 = (f32[2,6,256,128]{3,2,1,0:T(8,128)S(1)}, f32[2,6,256,128]{3,2,1,0:T(8,128)}, u32[]{:S(2)}) copy-start(f32[2,6,256,128]{3,2,1,0:T(8,128)} %get-tuple-element.401) | copy-start | bytes 4718596 | tf_op jit(solution)/shard_map/while/body/eval_jaxpr/cond
  295.9 1.1 copy-start.3
  297.8 8.6 %copy-start.2 = (f32[2,6,256,128]{3,2,1,0:T(8,128)S(1)}, f32[2,6,256,128]{3,2,1,0:T(8,128)}, u32[]{:S(2)}) copy-start(f32[2,6,256,128]{3,2,1,0:T(8,128)} %get-tuple-element.401) | copy-start | bytes 4718596 | tf_op jit(solution)/shard_map/while/body/eval_jaxpr/cond
  318.7 1.1 copy-start.3
  320.6 8.6 %copy-start.2 = (f32[2,6,256,128]{3,2,1,0:T(8,128)S(1)}, f32[2,6,256,128]{3,2,1,0:T(8,128)}, u32[]{:S(2)}) copy-start(f32[2,6,256,128]{3,2,1,0:T(8,128)} %get-tuple-element.401) | copy-start | bytes 4718596 | tf_op jit(solution)/shard_map/while/body/eval_jaxpr/cond
  343.3 8.6 %copy-start.2 = (f32[2,6,256,128]{3,2,1,0:T(8,128)S(1)}, f32[2,6,256,128]{3,2,1,0:T(8,128)}, u32[]{:S(2)}) copy-start(f32[2,6,256,128]{3,2,1,0:T(8,128)} %get-tuple-element.401) | copy-start | bytes 4718596 | tf_op jit(solution)/shard_map/while/body/eval_jaxpr/cond
  366.1 8.6 %copy-start.2 = (f32[2,6,256,128]{3,2,1,0:T(8,128)S(1)}, f32[2,6,256,128]{3,2,1,0:T(8,128)}, u32[]{:S(2)}) copy-start(f32[2,6,256,128]{3,2,1,0:T(8,128)} %get-tuple-element.401) | copy-start | bytes 4718596 | tf_op jit(solution)/shard_map/while/body/eval_jaxpr/cond
  388.8 8.6 %copy-start.2 = (f32[2,6,256,128]{3,2,1,0:T(8,128)S(1)}, f32[2,6,256,128]{3,2,1,0:T(8,128)}, u32[]{:S(2)}) copy-start(f32[2,6,256,128]{3,2,1,0:T(8,128)} %get-tuple-element.401) | copy-start | bytes 4718596 | tf_op jit(solution)/shard_map/while/body/eval_jaxpr/cond
  411.5 8.6 %copy-start.2 = (f32[2,6,256,128]{3,2,1,0:T(8,128)S(1)}, f32[2,6,256,128]{3,2,1,0:T(8,128)}, u32[]{:S(2)}) copy-start(f32[2,6,256,128]{3,2,1,0:T(8,128)} %get-tuple-element.401) | copy-start | bytes 4718596 | tf_op jit(solution)/shard_map/while/body/eval_jaxpr/cond
  432.4 1.1 copy-start.3
  434.3 8.6 %copy-start.2 = (f32[2,6,256,128]{3,2,1,0:T(8,128)S(1)}, f32[2,6,256,128]{3,2,1,0:T(8,128)}, u32[]{:S(2)}) copy-start(f32[2,6,256,128]{3,2,1,0:T(8,128)} %get-tuple-element.401) | copy-start | bytes 4718596 | tf_op jit(solution)/shard_map/while/body/eval_jaxpr/cond
  457.0 8.6 %copy-start.2 = (f32[2,6,256,128]{3,2,1,0:T(8,128)S(1)}, f32[2,6,256,128]{3,2,1,0:T(8,128)}, u32[]{:S(2)}) copy-start(f32[2,6,256,128]{3,2,1,0:T(8,128)} %get-tuple-element.401) | copy-start | bytes 4718596 | tf_op jit(solution)/shard_map/while/body/eval_jaxpr/cond
  479.8 8.6 %copy-start.2 = (f32[2,6,256,128]{3,2,1,0:T(8,128)S(1)}, f32[2,6,256,128]{3,2,1,0:T(8,128)}, u32[]{:S(2)}) copy-start(f32[2,6,256,128]{3,2,1,0:T(8,128)} %get-tuple-element.401) | copy-start | bytes 4718596 | tf_op jit(solution)/shard_map/while/body/eval_jaxpr/cond
  505.0 43.1 %copy-start.4 = (f32[256,1024]{1,0:T(8,128)S(1)}, f32[256,1024]{1,0:T(8,128)}, u32[]{:S(2)}) copy-start(f32[256,1024]{1,0:T(8,128)} %param.16) | copy-start | bytes 3145732
  546.9 18.5 %copy-start.5 = (f32[1024]{0:T(1024)S(1)}, f32[1024]{0:T(1024)}, u32[]{:S(2)}) copy-start(f32[1024]{0:T(1024)} %param.18) | copy-start | bytes 12292
  (7 other events, 8.0 us)
Sparse Core Ops, SparseCore 0:
  10.3 52.9 all-gather.5
  65.5 52.3 all-gather.7
  120.2 71.9 all-gather.9
where the time goes:
time: 577 us; the launch traced here: 573 us
  matrix products  322 us (56%)
  local copies, waits for them, and re-layouts  72.5 us (13%)
  blocking collectives  69.9 us (12%)
  other arithmetic  68.9 us (12%)
  between operations  14.5 us (3%)
  waiting for transfers between devices  13.6 us (2%)
  loops' own time  11.8 us (2%)
    dot_general x16, matrix products, attend(): jnp.einsum('kgts,skd->kgtd', weights, value_slab, precision=HIGHEST)  195 us
    dot_general x16, matrix products, attend(): jnp.einsum('tkgd,skd->kgts', query_rows, key_slab, precision=HIGHEST)  113 us
    unnamed x1, blocking collectives  59.2 us
    select_n x32, other arithmetic, turn(): return jax.tree.map(lambda a, b: jnp.where(reached, a, b), new, before)  37.5 us
    unnamed x16, local copies, waits for them, and re-layouts  25.6 us
    reduce_sum x16, other arithmetic, attend(): new_total = old_total * shrink + jnp.sum(weights, axis=3)  24 us
    cond x80, local copies, waits for them, and re-layouts  18.2 us
    all_gather x1, waiting for transfers between devices, soft_layer(): value_rows = lax.all_gather(v_soft, 'ctx', axis=0, tiled=True)  12.2 us
  transfers between devices with their start and end apart: 3, of which 1 were waited for; matrix products, arithmetic and copies ran while one was open for 69% of the time, Pallas kernels for 0%

commit v1 on v0

--- a/solution.py
+++ b/solution.py
@@ -73,8 +73,12 @@
             )
         )
     initial = tuple(initial)
-    key_rows = lax.all_gather(k_soft, "ctx", axis=0, tiled=True)
-    value_rows = lax.all_gather(v_soft, "ctx", axis=0, tiled=True)
+    derive_side = lambda local_values, local_x: jnp.split(
+        jax.lax.all_gather(jnp.concatenate([local_values, local_x], 1), "ctx", axis=0, tiled=True),
+        [local_values.shape[1]],
+        1,
+    )
+    key_rows, value_rows = derive_side(k_soft, v_soft)
     shard_rows = key_rows.shape[0]
     key_block = math.gcd(shard_rows, 512)
     key_rows = key_rows.reshape(shard_rows // key_block, key_block, kv_heads, HD)

time: 577 us -> 594 us (1.029)
  local copies, waits for them, and re-layouts: 72.5 us -> 82.3 us
    split x0 -> x1, local copies, waits for them, and re-layouts: none -> 11.5 us  [soft_layer(): jnp.split(jax.lax.all_gather(jnp.concatenate([local_values, local_x], 1),...]
    all_gather x2 -> x1, waiting for transfers between devices: 12.2 us -> 15.1 us  [soft_layer(): jax.lax.all_gather(jnp.concatenate([local_values, local_x], 1), 'ctx', ax...]
    unnamed x16 -> x18, local copies, waits for them, and re-layouts: 25.6 us -> 24.1 us
  transfers between devices with their start and end apart: 3 -> 2, of which waited for: 1 -> 1; matrix products, arithmetic and copies ran while one was open for 69% -> 10% of each run, Pallas kernels for 0% -> 0%
where the time goes in v1:
time: 594 us; the launch traced here: 590 us
  matrix products  322 us (54%)
  local copies, waits for them, and re-layouts  82.3 us (14%)
  other arithmetic  72.4 us (12%)
  blocking collectives  72.1 us (12%)
  waiting for transfers between devices  15.1 us (3%)
  between operations  14.8 us (2%)
  loops' own time  11.9 us (2%)
    dot_general x16, matrix products, attend(): jnp.einsum('kgts,skd->kgtd', weights, value_slab, precision=HIGHEST)  195 us
    dot_general x16, matrix products, attend(): jnp.einsum('tkgd,skd->kgts', query_rows, key_slab, precision=HIGHEST)  113 us
    unnamed x1, blocking collectives  60 us
    select_n x32, other arithmetic, turn(): return jax.tree.map(lambda a, b: jnp.where(reached, a, b), new, before)  37.8 us
    reduce_sum x16, other arithmetic, attend(): new_total = old_total * shrink + jnp.sum(weights, axis=3)  24.1 us
    unnamed x18, local copies, waits for them, and re-layouts  24.1 us
    cond x80, local copies, waits for them, and re-layouts  18.2 us
    all_gather x1, waiting for transfers between devices, soft_layer(): jax.lax.all_gather(jnp.concatenate([local_values, local_x], 1), 'ctx', ax...  15.1 us
  transfers between devices with their start and end apart: 2, of which 1 were waited for; matrix products, arithmetic and copies ran while one was open for 10% of the time, Pallas kernels for 0%

profile of v1, /device:TPU:30, one launch (start us, length us, event | category | flops | bytes accessed | tf_op | source)
XLA Modules:
  0.0 590.4 jit_solution(15811000384148834762)
XLA Ops:
  17.8 60.0 %all-reduce = f32[256]{0:T(256)S(1)} all-reduce(f32[256]{0:T(256)S(1)} %dynamic-update-slice), channel_id=2, replica_groups=mesh['ctx'=32,'head'=4] {'ctx'}, use_global_device_ids=true, to_apply=%add | all-reduce | flops 256 | bytes 2048
  87.8 39.1 %while.34 = (s32[]{:T(128)}, f32[8,128,128]{2,1,0:T(8,128)S(1)}, s32[]{:T(128)}, f32[32,8]{1,0:T(8,128)S(1)}, f32[32,8,128,128]{3,2,1,0:T(8,128)}, /*index=5*/s32[]{:T(128)}, s32[]{:T(128)}) while((s32[]{:T(128)}, f32[8,128,128]{2,1,0:T(8,128)S(1)}, s32[]{:T(128)}, f32[32,8]{1,0:T(8,128)S(1)}, f32[32,8,128,128]{3,2,1,0:T(8,128)}, ...), condition=%wide.region_3.4_spmd.clone, body=%wide.region_2.3_spmd.clone.sunk | while | flops 524292 | bytes 1573065 | solution.py:28
  146.1 15.1 %all-gather.5.cloned.1.call-done = f32[8192,512]{1,0:T(8,128)} async-done(((f32[256,512]{1,0:T(8,128)}), f32[8192,512]{1,0:T(8,128)}) %all-gather.5.cloned.1.call-update) | async-done | bytes 16777232 | tf_op jit(solution)/shard_map/all_gather | solution.py:77
  210.9 364.0 %while.33 = (s32[]{:T(128)}, f32[2,6,256]{2,1,0:T(8,128)S(1)}, f32[2,6,256]{2,1,0:T(8,128)S(1)}, f32[2,6,256,128]{3,2,1,0:T(8,128)}, s32[]{:T(128)}, /*index=5*/...) while((s32[]{:T(128)}, f32[2,6,256]{2,1,0:T(8,128)S(1)}, ...), condition=%wide.region_12.13_spmd.clone, body=%wide.region_7.0_spmd.clone.sunk | while | flops 4851637248 | bytes 37959000 | solution.py:106
  211.5 22.2 %conditional.3 = ((f32[2,6,256]{2,1,0:T(8,128)S(1)}, f32[2,6,256]{2,1,0:T(8,128)S(1)}, f32[2,6,256,128]{3,2,1,0:T(8,128)})) conditional(s32[]{:T(128)} %convert_element_type.10, (f32[2,6,256]{2,1,0:T(8,128)S(1)}, f32[2,6,256]{2,1,0:T(8,128)S(1)}, f32[2,6,256,128]{3,2,1,0:T(8,128)}) %tuple.99, (s32[]{:T(128)}, s32[512]{0:T(512)S(1)}, s32[]{:T(128)}, ...), branch_computations={%region_8.8_spmd, %region_9.11_spmd} | conditional | flops 4851637248 | bytes 37955680 | solution.py:103
  220.3 12.2 %multiply_add_fusion = f32[2,6,256,128]{3,2,1,0:T(8,128)S(1)} fusion(f32[2,6,256,128]{3,2,1,0:T(8,128)S(1)} %copy-done.3, f32[2,512,256,6]{2,1,3,0:T(8,128)S(1)} %get-tuple-element.535, f32[2,6,256]{2,1,0:T(8,128)S(1)} %max.6, pred[256,512]{0,1:T(8,128)(4,1)S(1)} %broadcast_compare_fusion, f32[2,6,256]{2,1,0:T(8,128)S(1)} %get-tuple-element.531, ...), kind=kOutput, calls=%fused_computation.11 | convolution fusion | flops 2422996992 | bytes 10117632 | tf_op jit(solution)/shard_map/while/body/eval_jaxpr/cond/branch_1_fun/kgts,skd->kgtd/dot_general | solution.py:57
  234.2 22.2 %conditional.3 = ((f32[2,6,256]{2,1,0:T(8,128)S(1)}, f32[2,6,256]{2,1,0:T(8,128)S(1)}, f32[2,6,256,128]{3,2,1,0:T(8,128)})) conditional(s32[]{:T(128)} %convert_element_type.10, (f32[2,6,256]{2,1,0:T(8,128)S(1)}, f32[2,6,256]{2,1,0:T(8,128)S(1)}, f32[2,6,256,128]{3,2,1,0:T(8,128)}) %tuple.99, (s32[]{:T(128)}, s32[512]{0:T(512)S(1)}, s32[]{:T(128)}, ...), branch_computations={%region_8.8_spmd, %region_9.11_spmd} | conditional | flops 4851637248 | bytes 37955680 | solution.py:103
  257.0 22.2 %conditional.3 = ((f32[2,6,256]{2,1,0:T(8,128)S(1)}, f32[2,6,256]{2,1,0:T(8,128)S(1)}, f32[2,6,256,128]{3,2,1,0:T(8,128)})) conditional(s32[]{:T(128)} %convert_element_type.10, (f32[2,6,256]{2,1,0:T(8,128)S(1)}, f32[2,6,256]{2,1,0:T(8,128)S(1)}, f32[2,6,256,128]{3,2,1,0:T(8,128)}) %tuple.99, (s32[]{:T(128)}, s32[512]{0:T(512)S(1)}, s32[]{:T(128)}, ...), branch_computations={%region_8.8_spmd, %region_9.11_spmd} | conditional | flops 4851637248 | bytes 37955680 | solution.py:103
  265.8 12.2 %multiply_add_fusion = f32[2,6,256,128]{3,2,1,0:T(8,128)S(1)} fusion(f32[2,6,256,128]{3,2,1,0:T(8,128)S(1)} %copy-done.3, f32[2,512,256,6]{2,1,3,0:T(8,128)S(1)} %get-tuple-element.535, f32[2,6,256]{2,1,0:T(8,128)S(1)} %max.6, pred[256,512]{0,1:T(8,128)(4,1)S(1)} %broadcast_compare_fusion, f32[2,6,256]{2,1,0:T(8,128)S(1)} %get-tuple-element.531, ...), kind=kOutput, calls=%fused_computation.11 | convolution fusion | flops 2422996992 | bytes 10117632 | tf_op jit(solution)/shard_map/while/body/eval_jaxpr/cond/branch_1_fun/kgts,skd->kgtd/dot_general | solution.py:57
  279.7 22.2 %conditional.3 = ((f32[2,6,256]{2,1,0:T(8,128)S(1)}, f32[2,6,256]{2,1,0:T(8,128)S(1)}, f32[2,6,256,128]{3,2,1,0:T(8,128)})) conditional(s32[]{:T(128)} %convert_element_type.10, (f32[2,6,256]{2,1,0:T(8,128)S(1)}, f32[2,6,256]{2,1,0:T(8,128)S(1)}, f32[2,6,256,128]{3,2,1,0:T(8,128)}) %tuple.99, (s32[]{:T(128)}, s32[512]{0:T(512)S(1)}, s32[]{:T(128)}, ...), branch_computations={%region_8.8_spmd, %region_9.11_spmd} | conditional | flops 4851637248 | bytes 37955680 | solution.py:103
  302.5 22.2 %conditional.3 = ((f32[2,6,256]{2,1,0:T(8,128)S(1)}, f32[2,6,256]{2,1,0:T(8,128)S(1)}, f32[2,6,256,128]{3,2,1,0:T(8,128)})) conditional(s32[]{:T(128)} %convert_element_type.10, (f32[2,6,256]{2,1,0:T(8,128)S(1)}, f32[2,6,256]{2,1,0:T(8,128)S(1)}, f32[2,6,256,128]{3,2,1,0:T(8,128)}) %tuple.99, (s32[]{:T(128)}, s32[512]{0:T(512)S(1)}, s32[]{:T(128)}, ...), branch_computations={%region_8.8_spmd, %region_9.11_spmd} | conditional | flops 4851637248 | bytes 37955680 | solution.py:103
  311.3 12.2 %multiply_add_fusion = f32[2,6,256,128]{3,2,1,0:T(8,128)S(1)} fusion(f32[2,6,256,128]{3,2,1,0:T(8,128)S(1)} %copy-done.3, f32[2,512,256,6]{2,1,3,0:T(8,128)S(1)} %get-tuple-element.535, f32[2,6,256]{2,1,0:T(8,128)S(1)} %max.6, pred[256,512]{0,1:T(8,128)(4,1)S(1)} %broadcast_compare_fusion, f32[2,6,256]{2,1,0:T(8,128)S(1)} %get-tuple-element.531, ...), kind=kOutput, calls=%fused_computation.11 | convolution fusion | flops 2422996992 | bytes 10117632 | tf_op jit(solution)/shard_map/while/body/eval_jaxpr/cond/branch_1_fun/kgts,skd->kgtd/dot_general | solution.py:57
  325.2 22.2 %conditional.3 = ((f32[2,6,256]{2,1,0:T(8,128)S(1)}, f32[2,6,256]{2,1,0:T(8,128)S(1)}, f32[2,6,256,128]{3,2,1,0:T(8,128)})) conditional(s32[]{:T(128)} %convert_element_type.10, (f32[2,6,256]{2,1,0:T(8,128)S(1)}, f32[2,6,256]{2,1,0:T(8,128)S(1)}, f32[2,6,256,128]{3,2,1,0:T(8,128)}) %tuple.99, (s32[]{:T(128)}, s32[512]{0:T(512)S(1)}, s32[]{:T(128)}, ...), branch_computations={%region_8.8_spmd, %region_9.11_spmd} | conditional | flops 4851637248 | bytes 37955680 | solution.py:103
  334.0 12.2 %multiply_add_fusion = f32[2,6,256,128]{3,2,1,0:T(8,128)S(1)} fusion(f32[2,6,256,128]{3,2,1,0:T(8,128)S(1)} %copy-done.3, f32[2,512,256,6]{2,1,3,0:T(8,128)S(1)} %get-tuple-element.535, f32[2,6,256]{2,1,0:T(8,128)S(1)} %max.6, pred[256,512]{0,1:T(8,128)(4,1)S(1)} %broadcast_compare_fusion, f32[2,6,256]{2,1,0:T(8,128)S(1)} %get-tuple-element.531, ...), kind=kOutput, calls=%fused_computation.11 | convolution fusion | flops 2422996992 | bytes 10117632 | tf_op jit(solution)/shard_map/while/body/eval_jaxpr/cond/branch_1_fun/kgts,skd->kgtd/dot_general | solution.py:57
  348.0 22.2 %conditional.3 = ((f32[2,6,256]{2,1,0:T(8,128)S(1)}, f32[2,6,256]{2,1,0:T(8,128)S(1)}, f32[2,6,256,128]{3,2,1,0:T(8,128)})) conditional(s32[]{:T(128)} %convert_element_type.10, (f32[2,6,256]{2,1,0:T(8,128)S(1)}, f32[2,6,256]{2,1,0:T(8,128)S(1)}, f32[2,6,256,128]{3,2,1,0:T(8,128)}) %tuple.99, (s32[]{:T(128)}, s32[512]{0:T(512)S(1)}, s32[]{:T(128)}, ...), branch_computations={%region_8.8_spmd, %region_9.11_spmd} | conditional | flops 4851637248 | bytes 37955680 | solution.py:103
  356.8 12.2 %multiply_add_fusion = f32[2,6,256,128]{3,2,1,0:T(8,128)S(1)} fusion(f32[2,6,256,128]{3,2,1,0:T(8,128)S(1)} %copy-done.3, f32[2,512,256,6]{2,1,3,0:T(8,128)S(1)} %get-tuple-element.535, f32[2,6,256]{2,1,0:T(8,128)S(1)} %max.6, pred[256,512]{0,1:T(8,128)(4,1)S(1)} %broadcast_compare_fusion, f32[2,6,256]{2,1,0:T(8,128)S(1)} %get-tuple-element.531, ...), kind=kOutput, calls=%fused_computation.11 | convolution fusion | flops 2422996992 | bytes 10117632 | tf_op jit(solution)/shard_map/while/body/eval_jaxpr/cond/branch_1_fun/kgts,skd->kgtd/dot_general | solution.py:57
  370.7 22.2 %conditional.3 = ((f32[2,6,256]{2,1,0:T(8,128)S(1)}, f32[2,6,256]{2,1,0:T(8,128)S(1)}, f32[2,6,256,128]{3,2,1,0:T(8,128)})) conditional(s32[]{:T(128)} %convert_element_type.10, (f32[2,6,256]{2,1,0:T(8,128)S(1)}, f32[2,6,256]{2,1,0:T(8,128)S(1)}, f32[2,6,256,128]{3,2,1,0:T(8,128)}) %tuple.99, (s32[]{:T(128)}, s32[512]{0:T(512)S(1)}, s32[]{:T(128)}, ...), branch_computations={%region_8.8_spmd, %region_9.11_spmd} | conditional | flops 4851637248 | bytes 37955680 | solution.py:103
  393.5 22.2 %conditional.3 = ((f32[2,6,256]{2,1,0:T(8,128)S(1)}, f32[2,6,256]{2,1,0:T(8,128)S(1)}, f32[2,6,256,128]{3,2,1,0:T(8,128)})) conditional(s32[]{:T(128)} %convert_element_type.10, (f32[2,6,256]{2,1,0:T(8,128)S(1)}, f32[2,6,256]{2,1,0:T(8,128)S(1)}, f32[2,6,256,128]{3,2,1,0:T(8,128)}) %tuple.99, (s32[]{:T(128)}, s32[512]{0:T(512)S(1)}, s32[]{:T(128)}, ...), branch_computations={%region_8.8_spmd, %region_9.11_spmd} | conditional | flops 4851637248 | bytes 37955680 | solution.py:103
  402.3 12.2 %multiply_add_fusion = f32[2,6,256,128]{3,2,1,0:T(8,128)S(1)} fusion(f32[2,6,256,128]{3,2,1,0:T(8,128)S(1)} %copy-done.3, f32[2,512,256,6]{2,1,3,0:T(8,128)S(1)} %get-tuple-element.535, f32[2,6,256]{2,1,0:T(8,128)S(1)} %max.6, pred[256,512]{0,1:T(8,128)(4,1)S(1)} %broadcast_compare_fusion, f32[2,6,256]{2,1,0:T(8,128)S(1)} %get-tuple-element.531, ...), kind=kOutput, calls=%fused_computation.11 | convolution fusion | flops 2422996992 | bytes 10117632 | tf_op jit(solution)/shard_map/while/body/eval_jaxpr/cond/branch_1_fun/kgts,skd->kgtd/dot_general | solution.py:57
  416.2 22.2 %conditional.3 = ((f32[2,6,256]{2,1,0:T(8,128)S(1)}, f32[2,6,256]{2,1,0:T(8,128)S(1)}, f32[2,6,256,128]{3,2,1,0:T(8,128)})) conditional(s32[]{:T(128)} %convert_element_type.10, (f32[2,6,256]{2,1,0:T(8,128)S(1)}, f32[2,6,256]{2,1,0:T(8,128)S(1)}, f32[2,6,256,128]{3,2,1,0:T(8,128)}) %tuple.99, (s32[]{:T(128)}, s32[512]{0:T(512)S(1)}, s32[]{:T(128)}, ...), branch_computations={%region_8.8_spmd, %region_9.11_spmd} | conditional | flops 4851637248 | bytes 37955680 | solution.py:103
  425.0 12.2 %multiply_add_fusion = f32[2,6,256,128]{3,2,1,0:T(8,128)S(1)} fusion(f32[2,6,256,128]{3,2,1,0:T(8,128)S(1)} %copy-done.3, f32[2,512,256,6]{2,1,3,0:T(8,128)S(1)} %get-tuple-element.535, f32[2,6,256]{2,1,0:T(8,128)S(1)} %max.6, pred[256,512]{0,1:T(8,128)(4,1)S(1)} %broadcast_compare_fusion, f32[2,6,256]{2,1,0:T(8,128)S(1)} %get-tuple-element.531, ...), kind=kOutput, calls=%fused_computation.11 | convolution fusion | flops 2422996992 | bytes 10117632 | tf_op jit(solution)/shard_map/while/body/eval_jaxpr/cond/branch_1_fun/kgts,skd->kgtd/dot_general | solution.py:57
  439.0 22.2 %conditional.3 = ((f32[2,6,256]{2,1,0:T(8,128)S(1)}, f32[2,6,256]{2,1,0:T(8,128)S(1)}, f32[2,6,256,128]{3,2,1,0:T(8,128)})) conditional(s32[]{:T(128)} %convert_element_type.10, (f32[2,6,256]{2,1,0:T(8,128)S(1)}, f32[2,6,256]{2,1,0:T(8,128)S(1)}, f32[2,6,256,128]{3,2,1,0:T(8,128)}) %tuple.99, (s32[]{:T(128)}, s32[512]{0:T(512)S(1)}, s32[]{:T(128)}, ...), branch_computations={%region_8.8_spmd, %region_9.11_spmd} | conditional | flops 4851637248 | bytes 37955680 | solution.py:103
  447.8 12.2 %multiply_add_fusion = f32[2,6,256,128]{3,2,1,0:T(8,128)S(1)} fusion(f32[2,6,256,128]{3,2,1,0:T(8,128)S(1)} %copy-done.3, f32[2,512,256,6]{2,1,3,0:T(8,128)S(1)} %get-tuple-element.535, f32[2,6,256]{2,1,0:T(8,128)S(1)} %max.6, pred[256,512]{0,1:T(8,128)(4,1)S(1)} %broadcast_compare_fusion, f32[2,6,256]{2,1,0:T(8,128)S(1)} %get-tuple-element.531, ...), kind=kOutput, calls=%fused_computation.11 | convolution fusion | flops 2422996992 | bytes 10117632 | tf_op jit(solution)/shard_map/while/body/eval_jaxpr/cond/branch_1_fun/kgts,skd->kgtd/dot_general | solution.py:57
  461.7 22.2 %conditional.3 = ((f32[2,6,256]{2,1,0:T(8,128)S(1)}, f32[2,6,256]{2,1,0:T(8,128)S(1)}, f32[2,6,256,128]{3,2,1,0:T(8,128)})) conditional(s32[]{:T(128)} %convert_element_type.10, (f32[2,6,256]{2,1,0:T(8,128)S(1)}, f32[2,6,256]{2,1,0:T(8,128)S(1)}, f32[2,6,256,128]{3,2,1,0:T(8,128)}) %tuple.99, (s32[]{:T(128)}, s32[512]{0:T(512)S(1)}, s32[]{:T(128)}, ...), branch_computations={%region_8.8_spmd, %region_9.11_spmd} | conditional | flops 4851637248 | bytes 37955680 | solution.py:103
  470.5 12.2 %multiply_add_fusion = f32[2,6,256,128]{3,2,1,0:T(8,128)S(1)} fusion(f32[2,6,256,128]{3,2,1,0:T(8,128)S(1)} %copy-done.3, f32[2,512,256,6]{2,1,3,0:T(8,128)S(1)} %get-tuple-element.535, f32[2,6,256]{2,1,0:T(8,128)S(1)} %max.6, pred[256,512]{0,1:T(8,128)(4,1)S(1)} %broadcast_compare_fusion, f32[2,6,256]{2,1,0:T(8,128)S(1)} %get-tuple-element.531, ...), kind=kOutput, calls=%fused_computation.11 | convolution fusion | flops 2422996992 | bytes 10117632 | tf_op jit(solution)/shard_map/while/body/eval_jaxpr/cond/branch_1_fun/kgts,skd->kgtd/dot_general | solution.py:57
  484.5 22.2 %conditional.3 = ((f32[2,6,256]{2,1,0:T(8,128)S(1)}, f32[2,6,256]{2,1,0:T(8,128)S(1)}, f32[2,6,256,128]{3,2,1,0:T(8,128)})) conditional(s32[]{:T(128)} %convert_element_type.10, (f32[2,6,256]{2,1,0:T(8,128)S(1)}, f32[2,6,256]{2,1,0:T(8,128)S(1)}, f32[2,6,256,128]{3,2,1,0:T(8,128)}) %tuple.99, (s32[]{:T(128)}, s32[512]{0:T(512)S(1)}, s32[]{:T(128)}, ...), branch_computations={%region_8.8_spmd, %region_9.11_spmd} | conditional | flops 4851637248 | bytes 37955680 | solution.py:103
  493.3 12.2 %multiply_add_fusion = f32[2,6,256,128]{3,2,1,0:T(8,128)S(1)} fusion(f32[2,6,256,128]{3,2,1,0:T(8,128)S(1)} %copy-done.3, f32[2,512,256,6]{2,1,3,0:T(8,128)S(1)} %get-tuple-element.535, f32[2,6,256]{2,1,0:T(8,128)S(1)} %max.6, pred[256,512]{0,1:T(8,128)(4,1)S(1)} %broadcast_compare_fusion, f32[2,6,256]{2,1,0:T(8,128)S(1)} %get-tuple-element.531, ...), kind=kOutput, calls=%fused_computation.11 | convolution fusion | flops 2422996992 | bytes 10117632 | tf_op jit(solution)/shard_map/while/body/eval_jaxpr/cond/branch_1_fun/kgts,skd->kgtd/dot_general | solution.py:57
  507.2 22.2 %conditional.3 = ((f32[2,6,256]{2,1,0:T(8,128)S(1)}, f32[2,6,256]{2,1,0:T(8,128)S(1)}, f32[2,6,256,128]{3,2,1,0:T(8,128)})) conditional(s32[]{:T(128)} %convert_element_type.10, (f32[2,6,256]{2,1,0:T(8,128)S(1)}, f32[2,6,256]{2,1,0:T(8,128)S(1)}, f32[2,6,256,128]{3,2,1,0:T(8,128)}) %tuple.99, (s32[]{:T(128)}, s32[512]{0:T(512)S(1)}, s32[]{:T(128)}, ...), branch_computations={%region_8.8_spmd, %region_9.11_spmd} | conditional | flops 4851637248 | bytes 37955680 | solution.py:103
  530.0 22.2 %conditional.3 = ((f32[2,6,256]{2,1,0:T(8,128)S(1)}, f32[2,6,256]{2,1,0:T(8,128)S(1)}, f32[2,6,256,128]{3,2,1,0:T(8,128)})) conditional(s32[]{:T(128)} %convert_element_type.10, (f32[2,6,256]{2,1,0:T(8,128)S(1)}, f32[2,6,256]{2,1,0:T(8,128)S(1)}, f32[2,6,256,128]{3,2,1,0:T(8,128)}) %tuple.99, (s32[]{:T(128)}, s32[512]{0:T(512)S(1)}, s32[]{:T(128)}, ...), branch_computations={%region_8.8_spmd, %region_9.11_spmd} | conditional | flops 4851637248 | bytes 37955680 | solution.py:103
  538.8 12.2 %multiply_add_fusion = f32[2,6,256,128]{3,2,1,0:T(8,128)S(1)} fusion(f32[2,6,256,128]{3,2,1,0:T(8,128)S(1)} %copy-done.3, f32[2,512,256,6]{2,1,3,0:T(8,128)S(1)} %get-tuple-element.535, f32[2,6,256]{2,1,0:T(8,128)S(1)} %max.6, pred[256,512]{0,1:T(8,128)(4,1)S(1)} %broadcast_compare_fusion, f32[2,6,256]{2,1,0:T(8,128)S(1)} %get-tuple-element.531, ...), kind=kOutput, calls=%fused_computation.11 | convolution fusion | flops 2422996992 | bytes 10117632 | tf_op jit(solution)/shard_map/while/body/eval_jaxpr/cond/branch_1_fun/kgts,skd->kgtd/dot_general | solution.py:57
  552.7 22.2 %conditional.3 = ((f32[2,6,256]{2,1,0:T(8,128)S(1)}, f32[2,6,256]{2,1,0:T(8,128)S(1)}, f32[2,6,256,128]{3,2,1,0:T(8,128)})) conditional(s32[]{:T(128)} %convert_element_type.10, (f32[2,6,256]{2,1,0:T(8,128)S(1)}, f32[2,6,256]{2,1,0:T(8,128)S(1)}, f32[2,6,256,128]{3,2,1,0:T(8,128)}) %tuple.99, (s32[]{:T(128)}, s32[512]{0:T(512)S(1)}, s32[]{:T(128)}, ...), branch_computations={%region_8.8_spmd, %region_9.11_spmd} | conditional | flops 4851637248 | bytes 37955680 | solution.py:103
  561.5 12.2 %multiply_add_fusion = f32[2,6,256,128]{3,2,1,0:T(8,128)S(1)} fusion(f32[2,6,256,128]{3,2,1,0:T(8,128)S(1)} %copy-done.3, f32[2,512,256,6]{2,1,3,0:T(8,128)S(1)} %get-tuple-element.535, f32[2,6,256]{2,1,0:T(8,128)S(1)} %max.6, pred[256,512]{0,1:T(8,128)(4,1)S(1)} %broadcast_compare_fusion, f32[2,6,256]{2,1,0:T(8,128)S(1)} %get-tuple-element.531, ...), kind=kOutput, calls=%fused_computation.11 | convolution fusion | flops 2422996992 | bytes 10117632 | tf_op jit(solution)/shard_map/while/body/eval_jaxpr/cond/branch_1_fun/kgts,skd->kgtd/dot_general | solution.py:57
  (344 shorter events, 342.0 us)
Async XLA Ops:
  7.2 76.3 %copy-start = (f32[256,1024]{1,0:T(8,128)S(1)}, f32[256,1024]{1,0:T(8,128)}, u32[]{:S(2)}) copy-start(f32[256,1024]{1,0:T(8,128)} %param.14) | copy-start | bytes 3145732
  7.2 9.1 %copy-start.6 = (u32[128]{0:T(128)S(1)}, u32[128]{0:T(128)}, u32[]{:S(2)}) copy-start(u32[128]{0:T(128)} %constant.131) | copy-start | bytes 1540
  7.2 80.6 %all-gather.7.cloned.1.call-start = ((), (), s32[]{:S(2)}) async-start(), calls=%async_computation.1 | async-start | bytes 17301504 | tf_op jit(solution)/shard_map/all_gather | solution.py:16
  10.7 70.9 %copy-start.2 = (f32[256,1024]{0,1:T(8,128)}, f32[256,1024]{0,1:T(8,128)S(1)}, u32[]{:S(2)}) copy-start(f32[256,1024]{0,1:T(8,128)S(1)} %copy.79) | copy-start | bytes 3145732
  14.3 146.9 %all-gather.5.cloned.1.call-start = ((), (), s32[]{:S(2)}) async-start(), calls=%async_computation | async-start | bytes 17301504 | tf_op jit(solution)/shard_map/all_gather | solution.py:77
  211.7 8.6 %copy-start.3 = (f32[2,6,256,128]{3,2,1,0:T(8,128)S(1)}, f32[2,6,256,128]{3,2,1,0:T(8,128)}, u32[]{:S(2)}) copy-start(f32[2,6,256,128]{3,2,1,0:T(8,128)} %get-tuple-element.401) | copy-start | bytes 4718596 | tf_op jit(solution)/shard_map/while/body/eval_jaxpr/cond
  232.5 1.1 copy-start.4
  234.4 8.6 %copy-start.3 = (f32[2,6,256,128]{3,2,1,0:T(8,128)S(1)}, f32[2,6,256,128]{3,2,1,0:T(8,128)}, u32[]{:S(2)}) copy-start(f32[2,6,256,128]{3,2,1,0:T(8,128)} %get-tuple-element.401) | copy-start | bytes 4718596 | tf_op jit(solution)/shard_map/while/body/eval_jaxpr/cond
  255.2 1.1 copy-start.4
  257.2 8.6 %copy-start.3 = (f32[2,6,256,128]{3,2,1,0:T(8,128)S(1)}, f32[2,6,256,128]{3,2,1,0:T(8,128)}, u32[]{:S(2)}) copy-start(f32[2,6,256,128]{3,2,1,0:T(8,128)} %get-tuple-element.401) | copy-start | bytes 4718596 | tf_op jit(solution)/shard_map/while/body/eval_jaxpr/cond
  278.0 1.1 copy-start.4
  279.9 8.6 %copy-start.3 = (f32[2,6,256,128]{3,2,1,0:T(8,128)S(1)}, f32[2,6,256,128]{3,2,1,0:T(8,128)}, u32[]{:S(2)}) copy-start(f32[2,6,256,128]{3,2,1,0:T(8,128)} %get-tuple-element.401) | copy-start | bytes 4718596 | tf_op jit(solution)/shard_map/while/body/eval_jaxpr/cond
  300.7 1.1 copy-start.4
  302.7 8.6 %copy-start.3 = (f32[2,6,256,128]{3,2,1,0:T(8,128)S(1)}, f32[2,6,256,128]{3,2,1,0:T(8,128)}, u32[]{:S(2)}) copy-start(f32[2,6,256,128]{3,2,1,0:T(8,128)} %get-tuple-element.401) | copy-start | bytes 4718596 | tf_op jit(solution)/shard_map/while/body/eval_jaxpr/cond
  323.5 1.1 copy-start.4
  325.4 8.6 %copy-start.3 = (f32[2,6,256,128]{3,2,1,0:T(8,128)S(1)}, f32[2,6,256,128]{3,2,1,0:T(8,128)}, u32[]{:S(2)}) copy-start(f32[2,6,256,128]{3,2,1,0:T(8,128)} %get-tuple-element.401) | copy-start | bytes 4718596 | tf_op jit(solution)/shard_map/while/body/eval_jaxpr/cond
  346.2 1.1 copy-start.4
  348.2 8.6 %copy-start.3 = (f32[2,6,256,128]{3,2,1,0:T(8,128)S(1)}, f32[2,6,256,128]{3,2,1,0:T(8,128)}, u32[]{:S(2)}) copy-start(f32[2,6,256,128]{3,2,1,0:T(8,128)} %get-tuple-element.401) | copy-start | bytes 4718596 | tf_op jit(solution)/shard_map/while/body/eval_jaxpr/cond
  369.0 1.1 copy-start.4
  370.9 8.6 %copy-start.3 = (f32[2,6,256,128]{3,2,1,0:T(8,128)S(1)}, f32[2,6,256,128]{3,2,1,0:T(8,128)}, u32[]{:S(2)}) copy-start(f32[2,6,256,128]{3,2,1,0:T(8,128)} %get-tuple-element.401) | copy-start | bytes 4718596 | tf_op jit(solution)/shard_map/while/body/eval_jaxpr/cond
  393.7 8.6 %copy-start.3 = (f32[2,6,256,128]{3,2,1,0:T(8,128)S(1)}, f32[2,6,256,128]{3,2,1,0:T(8,128)}, u32[]{:S(2)}) copy-start(f32[2,6,256,128]{3,2,1,0:T(8,128)} %get-tuple-element.401) | copy-start | bytes 4718596 | tf_op jit(solution)/shard_map/while/body/eval_jaxpr/cond
  416.4 8.6 %copy-start.3 = (f32[2,6,256,128]{3,2,1,0:T(8,128)S(1)}, f32[2,6,256,128]{3,2,1,0:T(8,128)}, u32[]{:S(2)}) copy-start(f32[2,6,256,128]{3,2,1,0:T(8,128)} %get-tuple-element.401) | copy-start | bytes 4718596 | tf_op jit(solution)/shard_map/while/body/eval_jaxpr/cond
  439.2 8.6 %copy-start.3 = (f32[2,6,256,128]{3,2,1,0:T(8,128)S(1)}, f32[2,6,256,128]{3,2,1,0:T(8,128)}, u32[]{:S(2)}) copy-start(f32[2,6,256,128]{3,2,1,0:T(8,128)} %get-tuple-element.401) | copy-start | bytes 4718596 | tf_op jit(solution)/shard_map/while/body/eval_jaxpr/cond
  461.9 8.6 %copy-start.3 = (f32[2,6,256,128]{3,2,1,0:T(8,128)S(1)}, f32[2,6,256,128]{3,2,1,0:T(8,128)}, u32[]{:S(2)}) copy-start(f32[2,6,256,128]{3,2,1,0:T(8,128)} %get-tuple-element.401) | copy-start | bytes 4718596 | tf_op jit(solution)/shard_map/while/body/eval_jaxpr/cond
  482.7 1.1 copy-start.4
  484.7 8.6 %copy-start.3 = (f32[2,6,256,128]{3,2,1,0:T(8,128)S(1)}, f32[2,6,256,128]{3,2,1,0:T(8,128)}, u32[]{:S(2)}) copy-start(f32[2,6,256,128]{3,2,1,0:T(8,128)} %get-tuple-element.401) | copy-start | bytes 4718596 | tf_op jit(solution)/shard_map/while/body/eval_jaxpr/cond
  507.4 8.6 %copy-start.3 = (f32[2,6,256,128]{3,2,1,0:T(8,128)S(1)}, f32[2,6,256,128]{3,2,1,0:T(8,128)}, u32[]{:S(2)}) copy-start(f32[2,6,256,128]{3,2,1,0:T(8,128)} %get-tuple-element.401) | copy-start | bytes 4718596 | tf_op jit(solution)/shard_map/while/body/eval_jaxpr/cond
  530.2 8.6 %copy-start.3 = (f32[2,6,256,128]{3,2,1,0:T(8,128)S(1)}, f32[2,6,256,128]{3,2,1,0:T(8,128)}, u32[]{:S(2)}) copy-start(f32[2,6,256,128]{3,2,1,0:T(8,128)} %get-tuple-element.401) | copy-start | bytes 4718596 | tf_op jit(solution)/shard_map/while/body/eval_jaxpr/cond
  551.0 1.1 copy-start.4
  552.9 8.6 %copy-start.3 = (f32[2,6,256,128]{3,2,1,0:T(8,128)S(1)}, f32[2,6,256,128]{3,2,1,0:T(8,128)}, u32[]{:S(2)}) copy-start(f32[2,6,256,128]{3,2,1,0:T(8,128)} %get-tuple-element.401) | copy-start | bytes 4718596 | tf_op jit(solution)/shard_map/while/body/eval_jaxpr/cond
  574.9 6.3 %copy-start.5 = (f32[1024]{0:T(1024)S(1)}, f32[1024]{0:T(1024)}, u32[]{:S(2)}) copy-start(f32[1024]{0:T(1024)} %param.18) | copy-start | bytes 12292
  574.9 8.7 %copy-start.1 = (f32[256,1024]{1,0:T(8,128)S(1)}, f32[256,1024]{1,0:T(8,128)}, u32[]{:S(2)}) copy-start(f32[256,1024]{1,0:T(8,128)} %param.14) | copy-start | bytes 3145732
  (7 other events, 8.0 us)
Sparse Core Ops, SparseCore 0:
  14.4 72.5 all-gather.6
  89.2 71.8 all-gather.4
